TPU v7x, 32 devices: a whole 2x2x4 slice. The times are simulated.
32 devices in a mesh: row: 8 (over y, x, core), col: 4 (over z).
Axes of the slice: x: 2, y: 2, z: 4, core: 2. Of those that a mesh axis runs over, the one named last changes fastest.
Arguments:
- sensitivity: float32 [16384, 16384], P('row', 'col'), as said below
- injection: float32 [16384, 1024], P('col', 'row'), may hold values from -6 to 6
- dispatch_now: float32 [16384, 1024], P('row', 'col'), may hold values from -3 to 3
- limit_class: int32 [16384], P('row'), may hold values from 0 to 15
- box_table: float32 [16], replicated, may hold values from 0.3 to 1.5
- owner_index: int32 [16384, 1], P('row'), may hold values from 0 to 7; in each aligned block of 2048 rows (0 to 2047, 2048 to 4095, ...) at most 768 rows name the same one
- member_slot: int32 [16384], P('row'), may hold values from 0 to 127
- agg_limit: float32 [1024], P('row'), may hold values from 0.5 to 4
Outputs:
- dispatch: float32 [16384, 1024], P('row', 'col')
- aggregate: float32 [1024, 1024], P('row', 'col')
Inputs may be any that keep to these rules, and one draw needn't show every extreme that they name: `sensitivity`: symmetric. `owner_index`: in each aligned block of 2048 inverters (those of one index of row) at most 768 have the same owner, and some owner has exactly 768 in some block.
All inputs are finite; a program needn't handle non-finite values.
Results may differ from a plain program's by a relative error of at most 0.000088.
Values sent between devices are 32-bit elements; how exact they have to be, the bound alone decides.
A program may use at most 128 MiB of HBM per device.

v0:
```python
import jax
import jax.numpy as jnp
from jax import lax
from jax.sharding import PartitionSpec as P

step_size = 0.1


def body(
    sensitivity,
    injection,
    dispatch_now,
    limit_class,
    box_table,
    owner_index,
    member_slot,
    agg_limit,
):
    row_count = sensitivity.shape[0]
    owners = lax.axis_size("row")
    partial_value = jnp.dot(
        sensitivity,
        lax.all_gather(injection, "row", axis=1, tiled=True),
        precision=lax.Precision.HIGHEST,
        preferred_element_type=jnp.float32,
    )
    gradient = 2.0 * lax.psum_scatter(partial_value, "col", scatter_dimension=1, tiled=True)
    classes = jnp.arange(box_table.shape[0], dtype=jnp.int32)
    box_bound = jnp.sum(
        jnp.where(limit_class[:, None] == classes[None, :], box_table[None, :], 0.0), axis=1
    )[:, None]
    stepped = jnp.clip(dispatch_now - step_size * gradient, -box_bound, box_bound)
    scen_width = stepped.shape[1]
    agg_dev = agg_limit.shape[0]
    target = owner_index[:, 0]
    limit_col = agg_limit[:, None]
    capacity = 3 * row_count // owners
    one_hot = (target[:, None] == jnp.arange(owners, dtype=jnp.int32)[None, :]).astype(jnp.int32)
    slot_rank = jnp.sum(jnp.cumsum(one_hot, axis=0) * one_hot, axis=1) - 1
    flat_slot = target * capacity + slot_rank
    outgoing = jnp.zeros((owners * capacity, scen_width), jnp.float32).at[flat_slot].set(stepped)
    tag_list = jnp.full((owners * capacity,), -1, jnp.int32).at[flat_slot].set(member_slot)
    received, got_tags = (
        lax.all_to_all(
            outgoing.reshape(owners, capacity, scen_width),
            "row",
            split_axis=0,
            concat_axis=0,
            tiled=True,
        ),
        lax.all_to_all(
            tag_list.reshape(owners, capacity), "row", split_axis=0, concat_axis=0, tiled=True
        ),
    )
    selector = (
        got_tags.reshape(-1)[None, :] == jnp.arange(agg_dev, dtype=jnp.int32)[:, None]
    ).astype(jnp.float32)
    total = jnp.dot(
        selector,
        received.reshape(-1, scen_width),
        precision=lax.Precision.HIGHEST,
        preferred_element_type=jnp.float32,
    )
    factor = limit_col / jnp.maximum(jnp.abs(total), limit_col)
    slot_factor = lax.dot_general(
        selector,
        factor,
        (((0,), (0,)), ((), ())),
        precision=lax.Precision.HIGHEST,
        preferred_element_type=jnp.float32,
    )
    returned = lax.all_to_all(
        slot_factor.reshape(owners, capacity, scen_width),
        "row",
        split_axis=0,
        concat_axis=0,
        tiled=True,
    )
    own_factor = returned.reshape(-1, scen_width)[flat_slot]
    aggregate = total * factor
    dispatch = stepped * own_factor
    return (dispatch, aggregate)


def solution(mesh):
    placed = (
        P("row", "col"),
        P("col", "row"),
        P("row", "col"),
        P("row"),
        P(),
        P("row", None),
        P("row"),
        P("row"),
    )
    return jax.shard_map(
        body,
        mesh=mesh,
        in_specs=placed,
        out_specs=(P("row", "col"), P("row", "col")),
        check_vma=False,
    )
```

profile of v0, /device:TPU:0, one launch (start us, length us, event | category | flops | bytes accessed | tf_op | source)
XLA Modules:
  0.0 558.1 jit_solution(14146623835312227774)
XLA Ops:
  7.2 0.0 all-gather.2.cloned.1.call-start
  7.2 0.7 all-gather.2.cloned.1.call-update
  7.9 0.0 reduce-scatter.2.cloned.1.call-start
  7.9 97.8 %all-gather.2.cloned.1.call-done = f32[4096,1024]{1,0:T(8,128)} async-done(((f32[4096,128]{1,0:T(8,128)}), f32[4096,1024]{1,0:T(8,128)}) %all-gather.2.cloned.1.call-update) | async-done | bytes 16777232 | tf_op jit(solution)/shard_map/all_gather | solution.py:23
  105.7 114.7 %fusion.14 = f32[2048,1024]{1,0:T(8,128)} fusion(f32[2048,4096]{1,0:T(8,128)} %param.8, f32[4096,1024]{1,0:T(8,128)} %all-gather.2.cloned.1.call-done), kind=kOutput, calls=%fused_computation.30 | convolution fusion | flops 103079215104 | bytes 58720256 | tf_op jit(solution)/shard_map/dot_general | solution.py:21
  220.4 0.0 copy-start.1
  220.4 0.0 copy-start.2
  220.4 0.0 copy-start.4
  220.4 0.0 copy-start
  220.4 0.0 reduce-scatter.2.cloned.1.call-update
  220.4 0.7 copy-done.1
  221.1 2.3 reduce-window.6
  223.4 0.3 slice_reduce_fusion
  223.7 0.2 reduce-window.9
  223.8 0.1 add_bitcast_fusion
  224.0 8.8 %scatter_custom_fusion = s32[6144]{0:T(1024)} fusion(s32[2048]{0:T(1024)S(1)} %bitcast.37, s32[2048]{0:T(1024)} %param.14, s32[]{:T(128)} %constant.8.clone.1), kind=kCustom, calls=%fused_computation.25 | custom fusion | bytes 25088 | tf_op jit(solution)/shard_map/scatter | solution.py:42
  232.8 3.3 all-to-all-start
  236.2 0.0 copy-done.2
  236.2 0.0 copy-done.4
  236.2 0.1 select_reduce_fusion
  236.3 128.8 %reduce-scatter.2.cloned.1.call-done = f32[2048,256]{1,0:T(8,128)} async-done(((f32[2048,1024]{1,0:T(8,128)}), f32[2048,256]{1,0:T(8,128)}) %reduce-scatter.2.cloned.1.call-update) | async-done | bytes 2097168 | tf_op jit(solution)/shard_map/reduce_scatter | solution.py:27
  365.1 0.0 copy-done
  365.1 13.5 %scatter_custom_fusion.1 = f32[6144,256]{1,0:T(8,128)} fusion(s32[2048]{0:T(1024)S(1)} %bitcast.38, f32[]{:T(128)} %constant.6.clone.1, f32[2048,256]{1,0:T(8,128)S(1)} %copy-done, f32[2048,256]{1,0:T(8,128)} %reduce-scatter.2.cloned.1.call-done, f32[2048]{0:T(1024)S(1)} %neg.8, f32[2048]{0:T(1024)S(1)} %select_reduce_fusion), kind=kCustom, calls=%fused_computation.3 | custom fusion | flops 2097152 | bytes 10502148 | tf_op jit(solution)/shard_map/scatter | solution.py:41
  378.6 0.0 all-to-all-done
  378.6 0.0 copy-start.3
  378.6 75.5 %all_to_all.19 = f32[8,768,256]{2,1,0:T(8,128)S(1)} all-to-all(f32[8,768,256]{2,1,0:T(8,128)} %bitcast.32), channel_id=1, replica_groups=mesh['row'=8,'col'=4] {'row'}, dimensions={0} | all-to-all | bytes 12582912 | tf_op jit(solution)/shard_map/all_to_all | solution.py:44
  454.1 0.0 copy-done.3
  454.1 3.3 fusion.6
  457.4 4.6 fusion.2
  462.0 4.7 all-to-all-start.2
  466.7 71.6 %all-to-all-done.2 = f32[8,768,256]{2,1,0:T(8,128)} async-done(((f32[8,768,256]{2,1,0:T(8,128)}), f32[8,768,256]{2,1,0:T(8,128)}, u32[]{:S(2)}, u32[]{:S(2)}) %all-to-all-start.2) | async-done | bytes 6291488 | tf_op jit(solution)/shard_map/all_to_all | solution.py:72
  538.3 9.4 %gather_fusion = f32[2048,256]{1,0:T(8,128)S(1)} fusion(f32[6144,256]{1,0:T(8,128)} %bitcast.10, s32[2048]{0:T(1024)S(1)} %broadcast_clamp_fusion), kind=kCustom, calls=%fused_computation | custom fusion | bytes 4202496 | tf_op jit(solution)/shard_map/gather | solution.py:79
  547.8 3.5 fusion.13
  (6 shorter events, 0.1 us)
Async XLA Ops:
  7.2 98.6 %all-gather.2.cloned.1.call-start = ((), (), s32[]{:S(2)}) async-start(), calls=%async_computation.4 | async-start | bytes 18874368 | tf_op jit(solution)/shard_map/all_gather | solution.py:23
  7.9 357.2 %reduce-scatter.2.cloned.1.call-start = ((), (), s32[]{:S(2)}) async-start(), calls=%async_computation.5 | async-start | bytes 10485760 | tf_op jit(solution)/shard_map/reduce_scatter | solution.py:27
  220.4 0.7 copy-start.1
  220.4 15.8 %copy-start.2 = (s32[2048]{0:T(1024)S(1)}, s32[2048]{0:T(1024)}, u32[]{:S(2)}) copy-start(s32[2048]{0:T(1024)} %param.11) | copy-start | bytes 24580
  220.4 15.8 %copy-start.4 = (f32[16]{0:T(128)S(1)}, f32[16]{0:T(128)}, u32[]{:S(2)}) copy-start(f32[16]{0:T(128)} %param.12) | copy-start | bytes 196
  220.4 144.7 %copy-start = (f32[2048,256]{1,0:T(8,128)S(1)}, f32[2048,256]{1,0:T(8,128)}, u32[]{:S(2)}) copy-start(f32[2048,256]{1,0:T(8,128)} %param.10) | copy-start | bytes 6291460
  232.8 145.8 %all-to-all-start = ((s32[8,1,768]{2,1,0:T(1,128)}), s32[8,1,768]{2,1,0:T(1,128)S(1)}, u32[]{:S(2)}, u32[]{:S(2)}) async-start(s32[8,1,768]{2,1,0:T(1,128)} %bitcast.5), calls=%async_computation.1 | async-start | bytes 49152 | tf_op jit(solution)/shard_map/all_to_all | solution.py:51
  378.6 75.5 %copy-start.3 = (f32[128]{0:T(128)S(1)}, f32[128]{0:T(128)}, u32[]{:S(2)}) copy-start(f32[128]{0:T(128)} %param.15) | copy-start | bytes 1540
  462.0 76.3 %all-to-all-start.2 = ((f32[8,768,256]{2,1,0:T(8,128)}), f32[8,768,256]{2,1,0:T(8,128)}, u32[]{:S(2)}, u32[]{:S(2)}) async-start(f32[8,768,256]{2,1,0:T(8,128)} %bitcast.30), calls=%async_computation.3 | async-start | bytes 12582912 | tf_op jit(solution)/shard_map/all_to_all | solution.py:72
Sparse Core Ops, SparseCore 0:
  9.9 95.8 all-gather.1
  220.6 144.4 reduce-scatter.1
where the time goes:
time: 559 us; the launch traced here: 558 us
  waiting for transfers between devices  299 us (53%)
  matrix products  123 us (22%)
  blocking collectives  75.5 us (14%)
  other arithmetic  19.7 us (4%)
  local copies, waits for them, and re-layouts  19.2 us (3%)
  between operations  14.1 us (3%)
  starting transfers between devices  8.15 us (1%)
    reduce_scatter x1, waiting for transfers between devices, body(): lax.psum_scatter(partial_value, 'col', scatter_dimension=1, tiled=True)  129 us
    dot_general x1, matrix products, body(): jnp.dot(sensitivity, lax.all_gather(injection, 'row', axis=1, tiled=True)...  115 us
    all_gather x1, waiting for transfers between devices, body(): lax.all_gather(injection, 'row', axis=1, tiled=True)  97.8 us
    all_to_all x1, blocking collectives, body(): lax.all_to_all(outgoing.reshape(owners, capacity, scen_width), 'row', spl...  75.5 us
    all_to_all x1, waiting for transfers between devices, body(): lax.all_to_all(slot_factor.reshape(owners, capacity, scen_width), 'row',...  71.6 us
    scatter x1, other arithmetic, body(): jnp.zeros((owners * capacity, scen_width), jnp.float32).at[flat_slot]  13.5 us
  transfers between devices with their start and end apart: 4, of which 3 were waited for; matrix products, arithmetic and copies ran while one was open for 5% of the time, Pallas kernels for 0%

commit v1 on v0

v1 whole, which is shorter than its diff:
```python
import jax
import jax.numpy as jnp
from jax import lax
from jax.sharding import PartitionSpec as P

step_size = 0.1


chunks = 4


def rounded(x):
    return lax.reduce_precision(x, exponent_bits=8, mantissa_bits=7)


def split3(x):
    hi = rounded(x)
    rest = x - hi
    mid = rounded(rest)
    return tuple(part.astype(jnp.bfloat16) for part in (hi, mid, rest - mid))


def body(
    sensitivity,
    injection,
    dispatch_now,
    limit_class,
    box_table,
    owner_index,
    member_slot,
    agg_limit,
):
    owners = lax.axis_size("row")
    agg_dev = agg_limit.shape[0]
    row_count = sensitivity.shape[0]
    injection_t = injection.T
    width = injection_t.shape[0] // chunks
    group = owners // lax.axis_size("col")
    gradients = []
    for chunk in range(chunks):
        part = injection_t[chunk * width : (chunk + 1) * width]
        part = lax.all_gather(part, "row", axis=0, tiled=True)
        partial_value = lax.dot_general(
            part,
            sensitivity,
            (((1,), (1,)), ((), ())),
            precision=lax.Precision.HIGH,
            preferred_element_type=jnp.float32,
        )
        summed = lax.psum_scatter(partial_value, "col", scatter_dimension=0, tiled=True)
        gradients.append(summed.reshape(group, width, row_count))
    gradient = 2.0 * jnp.concatenate(gradients, axis=1).reshape(-1, row_count).T
    classes = jnp.arange(box_table.shape[0], dtype=jnp.int32)
    box_bound = jnp.sum(
        jnp.where(limit_class[:, None] == classes[None, :], box_table[None, :], 0.0), axis=1
    )[:, None]
    stepped = jnp.clip(dispatch_now - step_size * gradient, -box_bound, box_bound)
    agg_id = owner_index[:, 0] * agg_dev + member_slot
    aggs = owners * agg_dev
    selector = (agg_id[None, :] == jnp.arange(aggs, dtype=jnp.int32)[:, None]).astype(jnp.bfloat16)

    def pick(left, parts, dims):
        return sum(
            lax.dot_general(left, part, (dims, ((), ())), preferred_element_type=jnp.float32)
            for part in parts
        )

    local = pick(selector, split3(stepped), ((1,), (0,)))
    total = lax.psum_scatter(local, "row", scatter_dimension=0, tiled=True)
    limit_col = agg_limit[:, None]
    factor = limit_col / jnp.maximum(jnp.abs(total), limit_col)
    aggregate = total * factor
    all_factor = lax.all_gather(factor, "row", axis=0, tiled=True)
    own_factor = pick(selector, split3(all_factor), ((0,), (0,)))
    return (stepped * own_factor, aggregate)


def solution(mesh):
    placed = (
        P("row", "col"),
        P("col", "row"),
        P("row", "col"),
        P("row"),
        P(),
        P("row", None),
        P("row"),
        P("row"),
    )
    return jax.shard_map(
        body,
        mesh=mesh,
        in_specs=placed,
        out_specs=(P("row", "col"), P("row", "col")),
        check_vma=False,
    )
```

time: 559 us -> 440 us (0.79)
  blocking collectives: 75.5 us -> 0 us
  matrix products: 123 us -> 95.5 us
  waiting for transfers between devices: 299 us -> 316 us
  local copies, waits for them, and re-layouts: 19.2 us -> 5.62 us
  other arithmetic: 19.7 us -> 6.87 us
  starting transfers between devices: 8.15 us -> 1.07 us
    all_to_all x1 -> x0, blocking collectives: 75.5 us -> none  [body(): lax.all_to_all(outgoing.reshape(owners, capacity, scen_width), 'row', spl...]
    all_to_all x2 -> x0, waiting for transfers between devices: 71.6 us -> none  [the longest x1 71.6 us: body(): lax.all_to_all(slot_factor.reshape(owners, capacity, scen_width), 'row',...]
    reduce_scatter x1 -> x5, waiting for transfers between devices: 129 us -> 198 us  [the longest x4 162 us: body(): lax.psum_scatter(partial_value, 'col', scatter_dimension=0, tiled=True)]
    dot_general x3 -> x10, matrix products: 123 us -> 95.5 us  [the longest x4 79.9 us: body(): lax.dot_general(part, sensitivity, (((1,), (1,)), ((), ())), precision=la...]
    all_gather x1 -> x5, waiting for transfers between devices: 97.8 us -> 116 us  [the longest x4 92.9 us: body(): part = lax.all_gather(part, 'row', axis=0, tiled=True)]
    scatter x1 -> x0, other arithmetic: 13.5 us -> none  [body(): jnp.zeros((owners * capacity, scen_width), jnp.float32).at[flat_slot]]
    gather x1 -> x0, local copies, waits for them, and re-layouts: 9.42 us -> none  [body(): own_factor = returned.reshape(-1, scen_width)[flat_slot]]
    scatter x1 -> x0, local copies, waits for them, and re-layouts: 8.8 us -> none  [body(): jnp.full((owners * capacity,), -1, jnp.int32).at[flat_slot].set(member_slot)]
  transfers between devices with their start and end apart: 4 -> 10, of which waited for: 3 -> 10; matrix products, arithmetic and copies ran while one was open for 5% -> 18% of each run, Pallas kernels for 0% -> 0%
where the time goes in v1:
time: 440 us
  waiting for transfers between devices  316 us (72%)
  matrix products  95.5 us (22%)
  between operations  14.3 us (3%)
  other arithmetic  6.87 us (2%)
  local copies, waits for them, and re-layouts  5.62 us (1%)
    reduce_scatter x4, waiting for transfers between devices, body(): lax.psum_scatter(partial_value, 'col', scatter_dimension=0, tiled=True)  162 us
    all_gather x4, waiting for transfers between devices, body(): part = lax.all_gather(part, 'row', axis=0, tiled=True)  92.9 us
    dot_general x4, matrix products, body(): lax.dot_general(part, sensitivity, (((1,), (1,)), ((), ())), precision=la...  79.9 us
    reduce_scatter x1, waiting for transfers between devices, body(): total = lax.psum_scatter(local, 'row', scatter_dimension=0, tiled=True)  35.2 us
    all_gather x1, waiting for transfers between devices, body(): all_factor = lax.all_gather(factor, 'row', axis=0, tiled=True)  23.6 us
    dot_general x6, matrix products, pick(): lax.dot_general(left, part, (dims, ((), ())), preferred_element_type=jnp....  15.6 us
  transfers between devices with their start and end apart: 10, of which 10 were waited for; matrix products, arithmetic and copies ran while one was open for 18% of the time, Pallas kernels for 0%

profile of v1, /device:TPU:0, one launch (start us, length us, event | category | flops | bytes accessed | tf_op | source)
XLA Modules:
  0.0 439.6 jit_solution(8798306970045158717)
XLA Ops:
  7.2 0.0 all-gather.6.cloned.1.call-start
  7.2 1.9 copy.13
  9.1 1.4 fusion.24
  10.5 0.0 all-gather.6.cloned.1.call-update
  10.5 0.0 all-gather.8.cloned.1.call-start
  10.6 0.7 all-gather.8.cloned.1.call-update
  11.3 0.0 all-gather.10.cloned.1.call-start
  11.3 0.7 all-gather.10.cloned.1.call-update
  12.0 0.0 all-gather.12.cloned.1.call-start
  12.1 0.5 all-gather.12.cloned.1.call-update
  12.6 0.0 reduce-scatter.6.cloned.1.call-start
  12.6 37.5 %all-gather.6.cloned.1.call-done = f32[256,4096]{1,0:T(8,128)} async-done(((f32[32,4096]{1,0:T(8,128)}), f32[256,4096]{1,0:T(8,128)}) %all-gather.6.cloned.1.call-update) | async-done | bytes 4194320 | tf_op jit(solution)/shard_map/all_gather | solution.py:42
  50.1 20.0 %fusion.25 = f32[256,2048]{1,0:T(8,128)} fusion(f32[256,4096]{1,0:T(8,128)} %all-gather.6.cloned.1.call-done, f32[2048,4096]{1,0:T(8,128)} %param.8), kind=kOutput, calls=%fused_computation.38 | convolution fusion | flops 12884901888 | bytes 39845888 | tf_op jit(solution)/shard_map/dot_general | solution.py:43
  70.1 0.0 reduce-scatter.6.cloned.1.call-update
  70.2 0.0 reduce-scatter.8.cloned.1.call-start
  70.2 18.6 %all-gather.8.cloned.1.call-done = f32[256,4096]{1,0:T(8,128)} async-done(((f32[32,4096]{1,0:T(8,128)}), f32[256,4096]{1,0:T(8,128)}) %all-gather.8.cloned.1.call-update) | async-done | bytes 4194320 | tf_op jit(solution)/shard_map/all_gather | solution.py:42
  88.8 20.0 %fusion.26 = f32[256,2048]{1,0:T(8,128)} fusion(f32[256,4096]{1,0:T(8,128)} %all-gather.8.cloned.1.call-done, f32[2048,4096]{1,0:T(8,128)} %param.8), kind=kOutput, calls=%fused_computation.39 | convolution fusion | flops 12884901888 | bytes 39845888 | tf_op jit(solution)/shard_map/dot_general | solution.py:43
  108.8 0.0 reduce-scatter.8.cloned.1.call-update
  108.9 0.2 reduce-scatter.10.cloned.1.call-start
  109.1 18.4 %all-gather.10.cloned.1.call-done = f32[256,4096]{1,0:T(8,128)} async-done(((f32[32,4096]{1,0:T(8,128)}), f32[256,4096]{1,0:T(8,128)}) %all-gather.10.cloned.1.call-update) | async-done | bytes 4194320 | tf_op jit(solution)/shard_map/all_gather | solution.py:42
  127.5 20.0 %fusion.27 = f32[256,2048]{1,0:T(8,128)} fusion(f32[256,4096]{1,0:T(8,128)} %all-gather.10.cloned.1.call-done, f32[2048,4096]{1,0:T(8,128)} %param.8), kind=kOutput, calls=%fused_computation.40 | convolution fusion | flops 12884901888 | bytes 39845888 | tf_op jit(solution)/shard_map/dot_general | solution.py:43
  147.5 0.0 reduce-scatter.10.cloned.1.call-update
  147.5 0.0 reduce-scatter.12.cloned.1.call-start
  147.5 18.4 %all-gather.12.cloned.1.call-done = f32[256,4096]{1,0:T(8,128)} async-done(((f32[32,4096]{1,0:T(8,128)}), f32[256,4096]{1,0:T(8,128)}) %all-gather.12.cloned.1.call-update) | async-done | bytes 4194320 | tf_op jit(solution)/shard_map/all_gather | solution.py:42
  166.0 19.8 %fusion.28 = f32[256,2048]{1,0:T(8,128)} fusion(f32[256,4096]{1,0:T(8,128)} %all-gather.12.cloned.1.call-done, f32[2048,4096]{1,0:T(8,128)} %param.8), kind=kOutput, calls=%fused_computation.41 | convolution fusion | flops 12884901888 | bytes 39845888 | tf_op jit(solution)/shard_map/dot_general | solution.py:43
  185.8 0.0 copy-start.3
  185.8 0.0 copy-start.6
  185.8 0.0 copy-start.4
  185.8 0.0 copy-start.2
  185.8 0.0 reduce-scatter.12.cloned.1.call-update
  185.8 0.3 reduce-scatter.14.cloned.1.call-start
  186.1 0.4 copy-done.3
  186.5 0.0 copy-done.6
  186.5 0.1 select_reduce_fusion
  186.6 0.0 copy-done.4
  186.6 0.0 copy-done.2
  186.7 25.3 %reduce-scatter.6.cloned.1.call-done = f32[64,2048]{1,0:T(8,128)} async-done(((f32[256,2048]{1,0:T(8,128)}), f32[64,2048]{1,0:T(8,128)}) %reduce-scatter.6.cloned.1.call-update) | async-done | bytes 524304 | tf_op jit(solution)/shard_map/reduce_scatter | solution.py:50
  212.0 45.5 %reduce-scatter.8.cloned.1.call-done = f32[64,2048]{1,0:T(8,128)} async-done(((f32[256,2048]{1,0:T(8,128)}), f32[64,2048]{1,0:T(8,128)}) %reduce-scatter.8.cloned.1.call-update) | async-done | bytes 524304 | tf_op jit(solution)/shard_map/reduce_scatter | solution.py:50
  257.5 45.5 %reduce-scatter.10.cloned.1.call-done = f32[64,2048]{1,0:T(8,128)} async-done(((f32[256,2048]{1,0:T(8,128)}), f32[64,2048]{1,0:T(8,128)}) %reduce-scatter.10.cloned.1.call-update) | async-done | bytes 524304 | tf_op jit(solution)/shard_map/reduce_scatter | solution.py:50
  303.0 46.2 %reduce-scatter.12.cloned.1.call-done = f32[64,2048]{1,0:T(8,128)} async-done(((f32[256,2048]{1,0:T(8,128)}), f32[64,2048]{1,0:T(8,128)}) %reduce-scatter.12.cloned.1.call-update) | async-done | bytes 524304 | tf_op jit(solution)/shard_map/reduce_scatter | solution.py:50
  349.2 3.1 maximum_multiply_fusion
  352.3 1.9 copy.15
  354.2 1.9 fusion.17
  356.2 0.0 copy-start
  356.2 1.7 fusion.3
  357.9 1.6 fusion.4
  359.5 0.0 copy-done
  359.5 0.0 copy-start.5
  359.5 2.5 fusion.19
  362.0 0.0 reduce-scatter.14.cloned.1.call-update
  362.0 0.3 all-gather.14.cloned.1.call-start
  362.4 35.2 %reduce-scatter.14.cloned.1.call-done = f32[128,256]{1,0:T(8,128)} async-done(((f32[1024,256]{1,0:T(8,128)}), f32[128,256]{1,0:T(8,128)}) %reduce-scatter.14.cloned.1.call-update) | async-done | bytes 131088 | tf_op jit(solution)/shard_map/reduce_scatter | solution.py:69
  397.6 0.0 copy-done.5
  397.6 1.7 fusion.23
  399.3 0.0 all-gather.14.cloned.1.call-update
  399.3 23.6 %all-gather.14.cloned.1.call-done = f32[1024,256]{1,0:T(8,128)} async-done(((f32[128,256]{1,0:T(8,128)}), f32[1024,256]{1,0:T(8,128)}) %all-gather.14.cloned.1.call-update) | async-done | bytes 1048592 | tf_op jit(solution)/shard_map/all_gather | solution.py:73
  422.9 0.0 copy-start.7
  422.9 3.7 fusion.1
  426.6 0.0 copy-done.7
  426.6 0.0 copy-start.1
  426.6 2.4 fusion.12
  429.0 0.0 copy-done.1
  429.1 3.7 fusion.14
  (3 shorter events, 0.0 us)
Async XLA Ops:
  7.2 42.9 %all-gather.6.cloned.1.call-start = ((), (), s32[]{:S(2)}) async-start(), calls=%async_computation.5 | async-start | bytes 4718592 | tf_op jit(solution)/shard_map/all_gather | solution.py:42
  10.5 78.3 %all-gather.8.cloned.1.call-start = ((), (), s32[]{:S(2)}) async-start(), calls=%async_computation.7 | async-start | bytes 4718592 | tf_op jit(solution)/shard_map/all_gather | solution.py:42
  11.3 116.2 %all-gather.10.cloned.1.call-start = ((), (), s32[]{:S(2)}) async-start(), calls=%async_computation.9 | async-start | bytes 4718592 | tf_op jit(solution)/shard_map/all_gather | solution.py:42
  12.0 154.0 %all-gather.12.cloned.1.call-start = ((), (), s32[]{:S(2)}) async-start(), calls=%async_computation.11 | async-start | bytes 4718592 | tf_op jit(solution)/shard_map/all_gather | solution.py:42
  12.6 199.4 %reduce-scatter.6.cloned.1.call-start = ((), (), s32[]{:S(2)}) async-start(), calls=%async_computation.6 | async-start | bytes 2621440 | tf_op jit(solution)/shard_map/reduce_scatter | solution.py:50
  70.2 187.3 %reduce-scatter.8.cloned.1.call-start = ((), (), s32[]{:S(2)}) async-start(), calls=%async_computation.8 | async-start | bytes 2621440 | tf_op jit(solution)/shard_map/reduce_scatter | solution.py:50
  108.9 194.1 %reduce-scatter.10.cloned.1.call-start = ((), (), s32[]{:S(2)}) async-start(), calls=%async_computation.10 | async-start | bytes 2621440 | tf_op jit(solution)/shard_map/reduce_scatter | solution.py:50
  147.5 201.7 %reduce-scatter.12.cloned.1.call-start = ((), (), s32[]{:S(2)}) async-start(), calls=%async_computation.12 | async-start | bytes 2621440 | tf_op jit(solution)/shard_map/reduce_scatter | solution.py:50
  185.8 0.7 copy-start.3
  185.8 0.7 copy-start.6
  185.8 0.8 copy-start.4
  185.8 0.8 copy-start.2
  185.8 211.7 %reduce-scatter.14.cloned.1.call-start = ((), (), s32[]{:S(2)}) async-start(), calls=%async_computation.13 | async-start | bytes 1179648 | tf_op jit(solution)/shard_map/reduce_scatter | solution.py:69
  356.2 3.3 copy-start
  359.5 38.1 %copy-start.5 = (f32[128]{0:T(128)S(1)}, f32[128]{0:T(128)}, u32[]{:S(2)}) copy-start(f32[128]{0:T(128)} %param.15) | copy-start | bytes 1540
  362.0 60.8 %all-gather.14.cloned.1.call-start = ((), (), s32[]{:S(2)}) async-start(), calls=%async_computation.14 | async-start | bytes 1179648 | tf_op jit(solution)/shard_map/all_gather | solution.py:73
  422.9 3.7 copy-start.7
  426.6 2.4 copy-start.1
Sparse Core Ops, SparseCore 0:
  10.6 39.4 all-gather.5
  52.0 36.7 all-gather.7
  90.7 36.7 all-gather.9
  129.2 36.7 all-gather.11
  168.1 43.8 reduce-scatter.5
  214.2 43.1 reduce-scatter.7
  259.8 43.1 reduce-scatter.9
  305.9 43.1 reduce-scatter.11
  362.2 35.3 reduce-scatter.13
  399.4 23.4 all-gather.13
